TPU v7x, 256 devices: a whole 4x4x8 slice. The times are simulated.
256 devices in a mesh: loop: 32 (over x_lo, z, core), row: 8 (over x_hi, y).
Axes of the slice: x: 4 (x_hi: 2, x_lo: 2; x = x_hi * 2 + x_lo), y: 4, z: 8, core: 2. Of those that a mesh axis runs over, the one named last changes fastest.
Arguments:
- start_pos: int32 [32], replicated, may hold values from 0 to 31, each once
- field_noise: float32 [32, 16, 256], replicated, may hold values from -5 to 5
- green_half: bfloat16 [512, 200, 1600], P('loop', None, 'row'), may hold values from -6 to 6
- orbitals: bfloat16 [512, 1600, 200], P('loop', 'row'), may hold values from -6 to 6
- rotated: bfloat16 [256, 200, 1600], P('loop', None, 'row'), may hold values from -0.009765625 to 0.009765625
- factors: bfloat16 [256, 1600, 1600], P('loop', 'row'), may hold values from -0.0546875 to 0.0546875
Outputs:
- propagated: float32 [512, 1600, 200], P('loop', 'row')
Inputs may be any that keep to these rules, and one draw needn't show every extreme that they name: `start_pos`: every loop position is the starting position of exactly one walker block.
All inputs are finite; a program needn't handle non-finite values.
Results may differ from a plain program's by a relative error of at most 0.0041.
Values may be sent and summed in bfloat16 or wider, within the bound.
A program may use at most 128 MiB of HBM per device.

v0:
```python
import jax
import jax.numpy as jnp
from jax import lax
from jax.sharding import PartitionSpec as P


def from_behind(array, axis, by):
    peers = lax.axis_size(axis)
    return lax.ppermute(array, axis, [(i, (i + by) % peers) for i in range(peers)])


def noise_rows(field_noise, start_pos, position, group, vec_width):
    block_total = start_pos.shape[0]
    block_id = jnp.sum(
        jnp.where(start_pos == position, jnp.arange(block_total, dtype=jnp.int32), 0)
    )
    noise_table = lax.dynamic_index_in_dim(field_noise, block_id, 0, keepdims=False)
    return lax.dynamic_slice_in_dim(noise_table, group * vec_width, vec_width, 1)


def stop_terms(green, rot_group, fac_group, orbit_full, noise_part):
    partial_bias = jnp.einsum("wip,gip->wg", green, rot_group, preferred_element_type=jnp.float32)
    force_bias = lax.psum(partial_bias, "row")
    shifted_field = (noise_part - force_bias).astype(jnp.bfloat16)
    operator = jnp.einsum(
        "wg,gpr->wpr", shifted_field, fac_group, preferred_element_type=jnp.float32
    ).astype(jnp.bfloat16)
    return jnp.einsum("wpr,wrn->wpn", operator, orbit_full, preferred_element_type=jnp.float32)


def body(start_pos, field_noise, green_half, orbitals, rotated, factors):
    loop_count = lax.axis_size("loop")
    position = lax.axis_index("loop")
    vec_width = rotated.shape[0]
    orbit_full = lax.all_gather(orbitals, "row", axis=1, tiled=True)
    resident_term = stop_terms(
        green_half,
        rotated,
        factors,
        orbit_full,
        noise_rows(field_noise, start_pos, position, position, vec_width),
    )
    prev_block = (position + loop_count - 1) % loop_count
    green_in, orbit_in = from_behind((green_half, orbit_full), "loop", 1)
    visit_term = stop_terms(
        green_in,
        rotated,
        factors,
        orbit_in,
        noise_rows(field_noise, start_pos, prev_block, position, vec_width),
    )
    returned = from_behind(visit_term, "loop", -1)
    return resident_term + returned


def solution(mesh):
    return jax.shard_map(
        body,
        mesh=mesh,
        in_specs=(
            P(),
            P(),
            P("loop", None, "row"),
            P("loop", "row", None),
            P("loop", None, "row"),
            P("loop", "row", None),
        ),
        out_specs=P("loop", "row", None),
        check_vma=False,
    )
```

profile of v0, /device:TPU:230, one launch (start us, length us, event | category | flops | bytes accessed | tf_op | source)
XLA Modules:
  0.0 408.3 jit_solution(1768400114232572445)
XLA Ops:
  6.5 0.0 copy-start
  6.5 0.0 all-gather.2.cloned.1.call-start
  6.5 0.7 all-gather.2.cloned.1.call-update
  7.3 0.0 copy-start.3
  7.3 0.0 copy-start.2
  7.3 156.3 %all-gather.2.cloned.1.call-done = bf16[16,1600,200]{2,1,0:T(8,128)(2,1)} async-done(((bf16[16,200,200]{2,1,0:T(8,128)(2,1)}), bf16[16,1600,200]{2,1,0:T(8,128)(2,1)}) %all-gather.2.cloned.1.call-update) | async-done | bytes 10240016 | tf_op jit(solution)/shard_map/all_gather | solution.py:35
  163.5 15.2 %copy.12 = bf16[16,1600,200]{1,2,0:T(8,128)(2,1)} copy(bf16[16,1600,200]{2,1,0:T(8,128)(2,1)} %all-gather.2.cloned.1.call-done) | data formatting | bytes 20480000 | tf_op jit(solution)/shard_map/all_gather | solution.py:35
  178.8 0.0 collective-permute-start.1
  178.8 0.0 copy-done.3
  178.8 0.0 collective-permute-start
  178.8 0.0 copy-done.2
  178.8 0.7 fusion.25
  183.6 0.8 constant_dynamic-slice_fusion
  184.4 0.1 copy.20
  184.4 0.0 copy-done
  184.4 0.7 fusion.10
  185.2 128.6 %collective-permute-done = bf16[16,200,200]{2,1,0:T(8,128)(2,1)} collective-permute-done((bf16[16,200,200]{2,1,0:T(8,128)(2,1)S(1)}, bf16[16,200,200]{2,1,0:T(8,128)(2,1)}, u32[]{:S(2)}, u32[]{:S(2)}) %collective-permute-start) | collective-permute-done | bytes 1280032 | tf_op jit(solution)/shard_map/ppermute | solution.py:9
  313.8 2.2 fusion.13
  315.9 21.6 %all-reduce = (f32[16,8]{0,1:T(8,128)S(1)}, f32[16,8]{0,1:T(8,128)S(1)}) all-reduce(f32[16,8]{0,1:T(8,128)S(1)} %fusion.10, f32[16,8]{0,1:T(8,128)S(1)} %fusion.13), channel_id=1, replica_groups=mesh['loop'=32,'row'=8] {'row'}, use_global_device_ids=true, to_apply=%region_1.2 | all-reduce | flops 256 | bytes 2048 | tf_op jit(solution)/shard_map/psum | solution.py:23
  337.5 9.1 %fusion.2 = bf16[16,200,1600]{2,0,1:T(8,128)(2,1)} fusion(bf16[8,200,1600]{2,1,0:T(8,128)(2,1)} %param.11, f32[16,8]{0,1:T(8,128)S(1)} %get-tuple-element.8, f32[1,16,8]{1,2,0:T(8,128)S(1)} %copy.20), kind=kOutput, calls=%fused_computation.4 | convolution fusion | flops 81920256 | bytes 15361024 | tf_op jit(solution)/shard_map/wg,gpr->wpr/dot_general | solution.py:25
  346.5 0.0 collective-permute-done.1
  346.5 14.4 %fusion.1 = f32[16,200,200]{2,1,0:T(8,128)} fusion(bf16[16,1600,200]{1,2,0:T(8,128)(2,1)} %collective-permute-done.1, bf16[16,200,1600]{2,0,1:T(8,128)(2,1)} %fusion.2), kind=kOutput, calls=%fused_computation.3 | convolution fusion | flops 2048000000 | bytes 23040000 | tf_op jit(solution)/shard_map/wpr,wrn->wpn/dot_general | solution.py:28
  360.9 0.0 collective-permute-start.2
  360.9 0.1 copy.19
  361.0 9.1 %fusion.4 = bf16[16,200,1600]{2,0,1:T(8,128)(2,1)} fusion(bf16[8,200,1600]{2,1,0:T(8,128)(2,1)} %param.11, f32[16,8]{0,1:T(8,128)S(1)} %get-tuple-element.7, f32[1,16,8]{1,2,0:T(8,128)S(1)} %copy.19), kind=kOutput, calls=%fused_computation.6 | convolution fusion | flops 81920256 | bytes 15361024 | tf_op jit(solution)/shard_map/wg,gpr->wpr/dot_general | solution.py:25
  370.1 0.0 copy-start.1
  370.1 11.1 %fusion = f32[16,200,200]{2,1,0:T(8,128)S(1)} fusion(bf16[16,1600,200]{2,1,0:T(8,128)(2,1)} %all-gather.2.cloned.1.call-done, bf16[16,200,1600]{2,0,1:T(8,128)(2,1)} %fusion.4), kind=kOutput, calls=%fused_computation.2 | convolution fusion | flops 2048000000 | bytes 23040000 | tf_op jit(solution)/shard_map/wpr,wrn->wpn/dot_general | solution.py:28
  381.2 16.2 %collective-permute-done.2 = f32[16,200,200]{2,1,0:T(8,128)} collective-permute-done((f32[16,200,200]{2,1,0:T(8,128)}, f32[16,200,200]{2,1,0:T(8,128)}, u32[]{:S(2)}, u32[]{:S(2)}) %collective-permute-start.2) | collective-permute-done | bytes 2560032 | tf_op jit(solution)/shard_map/ppermute | solution.py:9
  397.4 4.1 add.36
  401.5 0.0 copy-done.1
Async XLA Ops:
  6.5 177.9 %copy-start = (bf16[8,200,200]{2,1,0:T(8,128)(2,1)S(1)}, bf16[8,200,200]{2,1,0:T(8,128)(2,1)}, u32[]{:S(2)}) copy-start(bf16[8,200,200]{2,1,0:T(8,128)(2,1)} %param.10) | copy-start | bytes 1920004
  6.5 157.0 %all-gather.2.cloned.1.call-start = ((), (), s32[]{:S(2)}) async-start(), calls=%async_computation | async-start | bytes 14745600 | tf_op jit(solution)/shard_map/all_gather | solution.py:35
  7.3 171.5 %copy-start.3 = (bf16[16,200,200]{2,1,0:T(8,128)(2,1)S(1)}, bf16[16,200,200]{2,1,0:T(8,128)(2,1)}, u32[]{:S(2)}) copy-start(bf16[16,200,200]{2,1,0:T(8,128)(2,1)} %param.8) | copy-start | bytes 3840004
  7.3 171.5 %copy-start.2 = (s32[32]{0:T(128)S(1)}, s32[32]{0:T(128)}, u32[]{:S(2)}) copy-start(s32[32]{0:T(128)} %param.6) | copy-start | bytes 388
  178.8 167.8 %collective-permute-start.1 = (bf16[16,1600,200]{1,2,0:T(8,128)(2,1)}, bf16[16,1600,200]{1,2,0:T(8,128)(2,1)}, u32[]{:S(2)}, u32[]{:S(2)}) collective-permute-start(bf16[16,1600,200]{1,2,0:T(8,128)(2,1)} %copy.12), channel_id=1, source_target_pairs={{0,8},{8,16},{16,24},{24,32},{32,40},{40,48},{48,56},{56,64},{64,7... | collective-permute-start | bytes 30720008 | tf_op jit(solution)/shard_map/ppermute | solution.py:9
  178.8 135.0 %collective-permute-start = (bf16[16,200,200]{2,1,0:T(8,128)(2,1)S(1)}, bf16[16,200,200]{2,1,0:T(8,128)(2,1)}, u32[]{:S(2)}, u32[]{:S(2)}) collective-permute-start(bf16[16,200,200]{2,1,0:T(8,128)(2,1)S(1)} %copy-done.3), channel_id=1, source_target_pairs={{0,8},{8,16},{16,24},{24,32},{32,40},{40,48},{48,56},{56,64},{64,7... | collective-permute-start | bytes 3840008 | tf_op jit(solution)/shard_map/ppermute | solution.py:9
  360.9 36.5 %collective-permute-start.2 = (f32[16,200,200]{2,1,0:T(8,128)}, f32[16,200,200]{2,1,0:T(8,128)}, u32[]{:S(2)}, u32[]{:S(2)}) collective-permute-start(f32[16,200,200]{2,1,0:T(8,128)} %fusion.1), channel_id=1, source_target_pairs={{0,248},{8,0},{16,8},{24,16},{32,24},{40,32},{48,40},{56,48},{64,5... | collective-permute-start | bytes 7680008 | tf_op jit(solution)/shard_map/ppermute | solution.py:9
  370.1 31.4 %copy-start.1 = (bf16[8,200,200]{2,1,0:T(8,128)(2,1)S(1)}, bf16[8,200,200]{2,1,0:T(8,128)(2,1)}, u32[]{:S(2)}) copy-start(bf16[8,200,200]{2,1,0:T(8,128)(2,1)} %param.10) | copy-start | bytes 1920004
Sparse Core Ops, SparseCore 0:
  10.1 153.4 all-gather.1
where the time goes:
time: 415 us; the launch traced here: 408 us
  waiting for transfers between devices  302 us (73%)
  matrix products  46.5 us (11%)
  blocking collectives  21.6 us (5%)
  between operations  17.5 us (4%)
  local copies, waits for them, and re-layouts  16.2 us (4%)
  other arithmetic  4.77 us (1%)
    all_gather x1, waiting for transfers between devices, body(): orbit_full = lax.all_gather(orbitals, 'row', axis=1, tiled=True)  156 us
    ppermute x3, waiting for transfers between devices, from_behind(): lax.ppermute(array, axis, [(i, (i + by) % peers) for i in range(peers)])  145 us
    dot_general x2, matrix products, stop_terms(): jnp.einsum('wpr,wrn->wpn', operator, orbit_full, preferred_element_type=j...  25.4 us
    psum x1, blocking collectives, stop_terms(): force_bias = lax.psum(partial_bias, 'row')  21.6 us
    dot_general x2, matrix products, stop_terms(): jnp.einsum('wg,gpr->wpr', shifted_field, fac_group, preferred_element_typ...  18.2 us
    all_gather x1, local copies, waits for them, and re-layouts, body(): orbit_full = lax.all_gather(orbitals, 'row', axis=1, tiled=True)  15.2 us
  transfers between devices with their start and end apart: 4, of which 3 were waited for; matrix products, arithmetic and copies ran while one was open for 8% of the time, Pallas kernels for 0%

commit v1 on v0

v1 whole, which is shorter than its diff:
```python
import functools

import jax
import jax.numpy as jnp
from jax import lax
from jax.experimental import pallas as pl
from jax.experimental.pallas import tpu as pltpu
from jax.sharding import PartitionSpec as P

MESH = pl.DeviceIdType.MESH
F32, BF16 = jnp.float32, jnp.bfloat16
EXACT = lax.Precision.HIGHEST
LANE, TILE = 128, 16
SPLIT = (9, 4, 8, 4)
FAC_CUTS = (0, 512, 1024, 1536, 1600)
SHARD_ORDER = ((0, 0), (0, 1), (0, 3), (1, 0), (0, 2), (1, 1), (1, 3), (1, 2))


def same_slot(rows, cols, width):
    row = lax.broadcasted_iota(jnp.int32, (rows, cols), 0)
    col = lax.broadcasted_iota(jnp.int32, (rows, cols), 1)
    return lax.rem(row, width) == lax.rem(col, width)


def group_sum(rows, width):
    row = lax.broadcasted_iota(jnp.int32, (rows, LANE), 0)
    col = lax.broadcasted_iota(jnp.int32, (rows, LANE), 1)
    return (row // width == col // TILE).astype(F32)


def exact_dot(a, b):
    return lax.dot_general(a, b, (((1,), (0,)), ((), ())), precision=EXACT, preferred_element_type=F32)


def partial_bias(green, rot):
    walkers, nocc, width = green.shape
    vecs = rot.shape[0]
    whole = nocc // TILE
    left = nocc - whole * TILE

    def step(block, total):
        rows = pl.ds(pl.multiple_of(block * TILE, TILE), TILE)
        a = green[:, rows, :].reshape(walkers * TILE, width)
        b = rot[:, rows, :].reshape(vecs * TILE, width)
        return total + lax.dot_general(a, b, (((1,), (1,)), ((), ())), preferred_element_type=F32)

    total = lax.fori_loop(0, whole, step, jnp.zeros((walkers * TILE, vecs * TILE), F32))
    total = jnp.where(same_slot(walkers * TILE, vecs * TILE, TILE), total, 0.0)
    bias = exact_dot(total.reshape(walkers, TILE, vecs * TILE).sum(1), group_sum(vecs * TILE, TILE))
    if left:
        a = green[:, whole * TILE :, :].astype(F32).reshape(walkers * left, width).astype(BF16)
        b = rot[:, whole * TILE :, :].astype(F32).reshape(vecs * left, width).astype(BF16)
        rest = lax.dot_general(a, b, (((1,), (1,)), ((), ())), preferred_element_type=F32)
        rest = jnp.where(same_slot(walkers * left, vecs * left, left), rest, 0.0)
        bias += exact_dot(rest.reshape(walkers, left, vecs * left).sum(1), group_sum(vecs * left, left))
    return bias


def kernel(
    peers, start_pos, noise, green, orb, rot, fac, out,
    buf, orb_own, green_own, green_in, rot_own, fac_own, fac_in, oper, mix, mix_left, part, bias,
    own_sem, ag_send, ag_recv, fac_send, fac_recv, green_sem, bias_send, bias_recv,
):
    walkers, nrow, nocc = orb_own.shape
    vecs = rot_own.shape[0]
    l, r = lax.axis_index("loop"), lax.axis_index("row")
    half, y = r // 4, lax.rem(r, 4)

    def row(h, step):
        return lax.rem(half + h, 2) * 4 + lax.rem(y + step, 4)

    before, after = lax.rem(l + peers - 1, peers), lax.rem(l + 1, peers)
    up, down, across = (l, row(0, 1)), (l, row(0, 3)), (l, row(1, 0))

    loads = [
        pltpu.make_async_copy(src, dst, own_sem.at[i])
        for i, (src, dst) in enumerate(
            ((orb, orb_own), (green, green_own), (rot, rot_own), (fac, fac_own))
        )
    ]
    for load in loads:
        load.start()

    barrier = pltpu.get_barrier_semaphore()
    for d in range(1, 8):
        pl.semaphore_signal(barrier, inc=1, device_id=(l, lax.rem(r + d, 8)), device_id_type=MESH)
    for d in range(8):
        pl.semaphore_signal(barrier, inc=1, device_id=(after, lax.rem(r + d, 8)), device_id_type=MESH)
    pl.semaphore_signal(barrier, inc=1, device_id=(before, r), device_id_type=MESH)

    loads[0].wait()
    for w in range(walkers):
        buf[r, :, w * nocc : (w + 1) * nocc] = orb_own[w]
    pl.semaphore_wait(barrier, 16)

    sends = []

    def send(src, dst, send_sem, recv_sem, target):
        copy = pltpu.make_async_remote_copy(
            src_ref=src, dst_ref=dst, send_sem=send_sem, recv_sem=recv_sem,
            device_id=target, device_id_type=MESH,
        )
        copy.start()
        sends.append(copy)
        return copy

    a1, a2, b1, b2 = SPLIT
    pieces = {
        "A1": (0, a1), "A2": (a1, a2), "A": (0, a1 + a2),
        "B1": (a1 + a2, b1), "B2": (a1 + a2 + b1, b2), "B": (a1 + a2, b1 + b2),
    }
    used = [0]

    def pass_on(origin, piece, target):
        i = used[0]
        used[0] += 1
        first, count = pieces[piece]
        ref = buf.at[origin, :, pl.ds(first * LANE, count * LANE)]
        return send(ref, ref, ag_send.at[i], ag_recv.at[i], target)

    up_a, down_b = pass_on(r, "A", up), pass_on(r, "B", down)
    across_a, across_b = pass_on(r, "A", across), pass_on(r, "B", across)
    up_b, down_a = pass_on(r, "B", up), pass_on(r, "A", down)
    green_copy = send(green, green_in, green_sem.at[0], green_sem.at[1], (after, r))
    fac_copies = []
    for i in range(len(FAC_CUTS) - 1):
        cut = pl.ds(FAC_CUTS[i], FAC_CUTS[i + 1] - FAC_CUTS[i])
        fac_copies.append(
            send(fac.at[:, :, cut], fac_in.at[:, :, cut], fac_send.at[i], fac_recv.at[i], (before, r))
        )

    loads[1].wait()
    loads[2].wait()
    part[0] = partial_bias(green_own, rot_own)
    bias[0, r] = part[0]
    for d in range(1, 8):
        send(part.at[0], bias.at[0, r], bias_send.at[0, d], bias_recv.at[0, r], (l, lax.rem(r + d, 8)))

    up_a.wait_recv()
    pass_2 = pass_on(row(0, 3), "A2", up), pass_on(row(0, 3), "A1", up)
    pass_2x = pass_on(row(0, 3), "A1", across), pass_on(row(0, 3), "A2", across)
    down_b.wait_recv()
    pass_3 = pass_on(row(0, 1), "B2", down), pass_on(row(0, 1), "B1", down)
    pass_3x = pass_on(row(0, 1), "B1", across), pass_on(row(0, 1), "B2", across)
    across_a.wait_recv()
    pass_4m = pass_on(row(1, 0), "A", down)
    across_b.wait_recv()
    pass_4p = pass_on(row(1, 0), "B", up)

    green_copy.wait_recv()
    part[1] = partial_bias(green_in, rot_own)
    for d in range(8):
        send(part.at[1], bias.at[1, r], bias_send.at[1, d], bias_recv.at[1, r], (before, lax.rem(r + d, 8)))

    block = jnp.int32(0)
    for k in range(peers):
        block = jnp.where(start_pos[k] == l, jnp.int32(k), block)
    table = noise[block]
    columns = table.shape[1]
    row_id = lax.broadcasted_iota(jnp.int32, (columns, 2 * vecs * TILE), 0)
    col_id = lax.broadcasted_iota(jnp.int32, (columns, 2 * vecs * TILE), 1)
    pick = (row_id == lax.rem(l * vecs + col_id // TILE, columns)).astype(F32)
    noise_part = exact_dot(table, pick)

    pass_2x[0].wait_recv()
    pass_5 = pass_on(row(1, 3), "A1", up)
    pass_3x[0].wait_recv()
    pass_6 = pass_on(row(1, 1), "B1", down)
    pass_2[0].wait_recv()
    pass_7a = pass_on(row(0, 2), "A2", across)
    pass_3[0].wait_recv()
    pass_7b = pass_on(row(0, 2), "B2", across)

    for s in range(2):
        for d in range(1 - s, 8):
            j = lax.rem(r + d, 8)
            pltpu.make_async_remote_copy(
                src_ref=part.at[s], dst_ref=bias.at[s, j], send_sem=bias_send.at[s, d],
                recv_sem=bias_recv.at[s, j], device_id=across, device_id_type=MESH,
            ).wait_recv()
    sums = []
    for s in range(2):
        total = bias[s, 0]
        for j in range(1, 8):
            total += bias[s, j]
        sums.append(total)
    shifted = (noise_part - jnp.concatenate(sums, axis=1)).astype(BF16).astype(F32)
    depth = 2 * vecs * TILE
    spread = jnp.broadcast_to(shifted[:, None, :], (walkers, TILE, depth)).reshape(walkers * TILE, depth)
    mix[...] = jnp.where(same_slot(walkers * TILE, depth, TILE), spread, 0.0).astype(BF16)
    whole = nrow // TILE
    left = nrow - whole * TILE
    if left:
        row_id = lax.broadcasted_iota(jnp.int32, (depth, 2 * vecs * left), 0)
        col_id = lax.broadcasted_iota(jnp.int32, (depth, 2 * vecs * left), 1)
        few = exact_dot(shifted, (row_id == col_id // left * TILE).astype(F32))
        spread = jnp.broadcast_to(few[:, None, :], (walkers, left, 2 * vecs * left))
        spread = spread.reshape(walkers * left, 2 * vecs * left)
        mix_left[...] = jnp.where(same_slot(walkers * left, 2 * vecs * left, left), spread, 0.0).astype(BF16)

    def operator_of(shard):
        lanes = slice(shard * nrow, (shard + 1) * nrow)

        @pl.loop(0, whole)
        def _(block):
            rows = pl.ds(pl.multiple_of(block * TILE, TILE), TILE)
            both = jnp.concatenate(
                [f[:, rows, lanes].reshape(vecs * TILE, nrow) for f in (fac_own, fac_in)], axis=0
            )
            result = jnp.dot(mix[...], both, preferred_element_type=F32).astype(BF16)
            oper[shard, :, rows, :] = result.reshape(walkers, TILE, nrow)

        if left:
            rows = slice(whole * TILE, nrow)
            both = jnp.concatenate(
                [f[:, rows, lanes].astype(F32).reshape(vecs * left, nrow) for f in (fac_own, fac_in)], axis=0
            ).astype(BF16)
            result = jnp.dot(mix_left[...], both, preferred_element_type=F32)
            oper[shard, :, rows, :] = result.reshape(walkers, left, nrow).astype(BF16)

    loads[3].wait()
    done = 0
    for i, copy in enumerate(fac_copies):
        copy.wait_recv()
        while done < 8 and (done + 1) * nrow <= FAC_CUTS[i + 1]:
            operator_of(done)
            done += 1

    def apply(shard, first):
        for w in range(walkers):
            product = jnp.dot(
                oper[shard, w, 0:nrow, :],
                buf[shard, :, w * nocc : (w + 1) * nocc],
                preferred_element_type=F32,
            )
            out[w] = product if first else out[w] + product

    apply(r, True)
    for copy in (up_b, down_a, *pass_2[1:], *pass_3[1:], pass_4m, pass_4p, *pass_2x[1:], *pass_3x[1:]):
        copy.wait_recv()

    @pl.loop(1, 7)
    def _(step):
        over = step // 4
        along = lax.rem(step, 4) + step // 6
        apply(row(over, along), False)

    for copy in (pass_5, pass_6, pass_7a, pass_7b):
        copy.wait_recv()
    apply(row(1, 2), False)
    for copy in sends:
        copy.wait_send()


def body(start_pos, field_noise, green_half, orbitals, rotated, factors):
    peers = lax.axis_size("loop")
    walkers, nrow, nocc = orbitals.shape
    vecs, _, norb = factors.shape
    width = green_half.shape[2]
    left = nrow % TILE
    dma = pltpu.SemaphoreType.DMA
    vmem, hbm = pl.BlockSpec(memory_space=pltpu.VMEM), pl.BlockSpec(memory_space=pl.ANY)
    return pl.pallas_call(
        functools.partial(kernel, peers),
        out_shape=jax.ShapeDtypeStruct((walkers, nrow, nocc), F32),
        in_specs=[pl.BlockSpec(memory_space=pltpu.SMEM), vmem, hbm, hbm, hbm, hbm],
        out_specs=vmem,
        scratch_shapes=[
            pltpu.VMEM((8, nrow, walkers * nocc), BF16),
            pltpu.VMEM((walkers, nrow, nocc), BF16),
            pltpu.VMEM((walkers, nocc, width), BF16),
            pltpu.VMEM((walkers, nocc, width), BF16),
            pltpu.VMEM((vecs, nocc, width), BF16),
            pltpu.VMEM((vecs, nrow, norb), BF16),
            pltpu.VMEM((vecs, nrow, norb), BF16),
            pltpu.VMEM((8, walkers, nrow, nrow), BF16),
            pltpu.VMEM((walkers * TILE, 2 * vecs * TILE), BF16),
            pltpu.VMEM((walkers * left, 2 * vecs * left), BF16),
            pltpu.VMEM((2, walkers, LANE), F32),
            pltpu.VMEM((2, 8, walkers, LANE), F32),
            dma((4,)),
            dma((24,)),
            dma((24,)),
            dma((4,)),
            dma((4,)),
            dma((2,)),
            dma((2, 8)),
            dma((2, 8)),
        ],
        compiler_params=pltpu.CompilerParams(
            collective_id=0, has_side_effects=True, vmem_limit_bytes=60 * 2**20
        ),
        cost_estimate=pl.CostEstimate(
            flops=8 * walkers * nrow * norb * nocc, bytes_accessed=2 * 10**7, transcendentals=0
        ),
    )(start_pos, field_noise, green_half, orbitals, rotated, factors)


def solution(mesh):
    return jax.shard_map(
        body,
        mesh=mesh,
        in_specs=(
            P(),
            P(),
            P("loop", None, "row"),
            P("loop", "row", None),
            P("loop", None, "row"),
            P("loop", "row", None),
        ),
        out_specs=P("loop", "row", None),
        check_vma=False,
    )
```

time: 415 us -> 162 us (0.39); the launches traced: 408 us -> 162 us
  waiting for transfers between devices: 302 us -> 0 us
  Pallas kernels: 0 us -> 158 us
  matrix products: 46.5 us -> 0 us
  blocking collectives: 21.6 us -> 0 us
  between operations: 17.5 us -> 0.01 us
  local copies, waits for them, and re-layouts: 16.2 us -> 3.89 us
  other arithmetic: 4.77 us -> 0 us
    pallas_call x0 -> x1, Pallas kernels: none -> 158 us  [body(): pl.pallas_call(functools.partial(kernel, peers), out_shape=jax.ShapeDtype...]
    all_gather x1 -> x0, waiting for transfers between devices: 156 us -> none  [body(): orbit_full = lax.all_gather(orbitals, 'row', axis=1, tiled=True)]
    ppermute x3 -> x0, waiting for transfers between devices: 145 us -> none  [from_behind(): lax.ppermute(array, axis, [(i, (i + by) % peers) for i in range(peers)])]
    dot_general x6 -> x0, matrix products: 46.5 us -> none  [the longest x2 25.4 us: stop_terms(): jnp.einsum('wpr,wrn->wpn', operator, orbit_full, preferred_element_type=j...]
    psum x1 -> x0, blocking collectives: 21.6 us -> none  [stop_terms(): force_bias = lax.psum(partial_bias, 'row')]
    all_gather x1 -> x0, local copies, waits for them, and re-layouts: 15.2 us -> none  [body(): orbit_full = lax.all_gather(orbitals, 'row', axis=1, tiled=True)]
  transfers between devices with their start and end apart: 4 -> 0, of which waited for: 3 -> 0; matrix products, arithmetic and copies ran while one was open for 8% -> 0% of each run, Pallas kernels for 0% -> 0%
where the time goes in v1:
time: 162 us
  Pallas kernels  158 us (98%)
  local copies, waits for them, and re-layouts  3.89 us (2%)
    pallas_call x1, Pallas kernels, body(): pl.pallas_call(functools.partial(kernel, peers), out_shape=jax.ShapeDtype...  158 us
    unnamed x1, local copies, waits for them, and re-layouts  3.89 us

profile of v1, /device:TPU:230, one launch (start us, length us, event | category | flops | bytes accessed | tf_op | source)
XLA Modules:
  0.0 162.4 jit_solution(5500852643333398205)
XLA Ops:
  0.0 158.5 %shard_map.64 = f32[16,200,200]{2,1,0:T(8,128)} custom-call(s32[32]{0:T(128)} %start_pos.1, f32[32,16,256]{2,1,0:T(8,128)} %noise.1, bf16[16,200,200]{2,1,0:T(8,128)(2,1)} %green.1, bf16[16,200,200]{2,1,0:T(8,128)(2,1)} %orb.1, bf16[8,200,200]{2,1,0:T(8,128)(2,1)} %rot.1, bf16[8,200,1600]{2,1,0:T(8,128)(2,1)} %fac.1), custom_call_target="tpu_custom_call" | custom-call | flops 8192000000 | bytes 20000000 | tf_op jit(solution)/shard_map/pallas_call | solution.py:263
  158.5 3.9 %copy.8 = f32[16,200,200]{2,1,0:T(8,128)} copy(f32[16,200,200]{2,1,0:T(8,128)} %shard_map.64) | data formatting | bytes 5120000

commit v2 on v1

--- a/solution.py
+++ b/solution.py
@@ -11,9 +11,8 @@
 F32, BF16 = jnp.float32, jnp.bfloat16
 EXACT = lax.Precision.HIGHEST
 LANE, TILE = 128, 16
-SPLIT = (9, 4, 8, 4)
-FAC_CUTS = (0, 512, 1024, 1536, 1600)
-SHARD_ORDER = ((0, 0), (0, 1), (0, 3), (1, 0), (0, 2), (1, 1), (1, 3), (1, 2))
+PARTS = 4
+RELAY_Z = (0, 3, 4)
 
 
 def same_slot(rows, cols, width):
@@ -58,8 +57,8 @@
 
 def kernel(
     peers, start_pos, noise, green, orb, rot, fac, out,
-    buf, orb_own, green_own, green_in, rot_own, fac_own, fac_in, oper, mix, mix_left, part, bias,
-    own_sem, ag_send, ag_recv, fac_send, fac_recv, green_sem, bias_send, bias_recv,
+    buf, orb_own, green_own, green_in, rot_own, fac_own, fac_in, fac_relay, oper, mix, mix_left, part, bias,
+    own_sem, ag_send, ag_recv, fac_send, fac_recv, relay_sem, green_sem, bias_send, bias_recv,
 ):
     walkers, nrow, nocc = orb_own.shape
     vecs = rot_own.shape[0]
@@ -71,6 +70,12 @@
 
     before, after = lax.rem(l + peers - 1, peers), lax.rem(l + 1, peers)
     up, down, across = (l, row(0, 1)), (l, row(0, 3)), (l, row(1, 0))
+
+    turn = peers // 2
+    near, far = (l // turn) * turn, lax.rem((l // turn) * turn + turn, peers)
+    place = lax.rem(l, turn)
+    is_source, is_last = place == 0, place == turn - 1
+    is_relay = functools.reduce(jnp.logical_or, [place == 2 * z for z in RELAY_Z])
 
     loads = [
         pltpu.make_async_copy(src, dst, own_sem.at[i])
@@ -88,10 +93,20 @@
         pl.semaphore_signal(barrier, inc=1, device_id=(after, lax.rem(r + d, 8)), device_id_type=MESH)
     pl.semaphore_signal(barrier, inc=1, device_id=(before, r), device_id_type=MESH)
 
+    @pl.when(is_relay)
+    def _():
+        pl.semaphore_signal(barrier, inc=1, device_id=(far, r), device_id_type=MESH)
+
+    @pl.when(is_last)
+    def _():
+        for z in RELAY_Z:
+            pl.semaphore_signal(barrier, inc=1, device_id=(near + 2 * z, r), device_id_type=MESH)
+
     loads[0].wait()
     for w in range(walkers):
         buf[r, :, w * nocc : (w + 1) * nocc] = orb_own[w]
-    pl.semaphore_wait(barrier, 16)
+    targets = 16 + jnp.where(is_relay, 1, 0) + jnp.where(is_source, len(RELAY_Z), 0)
+    pl.semaphore_wait(barrier, targets)
 
     sends = []
 
@@ -104,11 +119,8 @@
         sends.append(copy)
         return copy
 
-    a1, a2, b1, b2 = SPLIT
-    pieces = {
-        "A1": (0, a1), "A2": (a1, a2), "A": (0, a1 + a2),
-        "B1": (a1 + a2, b1), "B2": (a1 + a2 + b1, b2), "B": (a1 + a2, b1 + b2),
-    }
+    tiles = walkers * nocc // LANE
+    pieces = {"A": (0, (tiles + 1) // 2), "B": ((tiles + 1) // 2, tiles // 2)}
     used = [0]
 
     def pass_on(origin, piece, target):
@@ -122,12 +134,31 @@
     across_a, across_b = pass_on(r, "A", across), pass_on(r, "B", across)
     up_b, down_a = pass_on(r, "B", up), pass_on(r, "A", down)
     green_copy = send(green, green_in, green_sem.at[0], green_sem.at[1], (after, r))
-    fac_copies = []
-    for i in range(len(FAC_CUTS) - 1):
-        cut = pl.ds(FAC_CUTS[i], FAC_CUTS[i + 1] - FAC_CUTS[i])
-        fac_copies.append(
-            send(fac.at[:, :, cut], fac_in.at[:, :, cut], fac_send.at[i], fac_recv.at[i], (before, r))
+
+    share = vecs // PARTS
+
+    def fac_copy(i, dst, recv_sem, target):
+        return pltpu.make_async_remote_copy(
+            src_ref=fac.at[pl.ds(i * share, share)], dst_ref=dst, send_sem=fac_send.at[i], recv_sem=recv_sem,
+            device_id=target, device_id_type=MESH,
         )
+
+    def landing(i):
+        return fac_in.at[pl.ds(i * share, share)]
+
+    fac_copies = [fac_copy(i, landing(i), fac_recv.at[i], (before, r)) for i in range(PARTS)]
+
+    @pl.when(is_source)
+    def _():
+        for i, z in enumerate(RELAY_Z, 1):
+            fac_copy(i, fac_relay, relay_sem.at[0], (far + 2 * z, r)).start()
+
+    fac_copies[0].start()
+
+    @pl.when(jnp.logical_not(is_source))
+    def _():
+        for copy in fac_copies[1:]:
+            copy.start()
 
     loads[1].wait()
     loads[2].wait()
@@ -137,15 +168,29 @@
         send(part.at[0], bias.at[0, r], bias_send.at[0, d], bias_recv.at[0, r], (l, lax.rem(r + d, 8)))
 
     up_a.wait_recv()
-    pass_2 = pass_on(row(0, 3), "A2", up), pass_on(row(0, 3), "A1", up)
-    pass_2x = pass_on(row(0, 3), "A1", across), pass_on(row(0, 3), "A2", across)
+    pass_2, pass_2x = pass_on(row(0, 3), "A", up), pass_on(row(0, 3), "A", across)
     down_b.wait_recv()
-    pass_3 = pass_on(row(0, 1), "B2", down), pass_on(row(0, 1), "B1", down)
-    pass_3x = pass_on(row(0, 1), "B1", across), pass_on(row(0, 1), "B2", across)
+    pass_3, pass_3x = pass_on(row(0, 1), "B", down), pass_on(row(0, 1), "B", across)
     across_a.wait_recv()
     pass_4m = pass_on(row(1, 0), "A", down)
     across_b.wait_recv()
     pass_4p = pass_on(row(1, 0), "B", up)
+
+    def relayed(i):
+        return pltpu.make_async_remote_copy(
+            src_ref=fac_relay, dst_ref=landing(i), send_sem=relay_sem.at[1], recv_sem=fac_recv.at[i],
+            device_id=(near + turn - 1, r), device_id_type=MESH,
+        )
+
+    @pl.when(is_relay)
+    def _():
+        fac_copy(1, fac_relay, relay_sem.at[0], across).wait_recv()
+
+    for i, z in enumerate(RELAY_Z, 1):
+
+        @pl.when(place == 2 * z)
+        def _():
+            relayed(i).start()
 
     green_copy.wait_recv()
     part[1] = partial_bias(green_in, rot_own)
@@ -162,14 +207,10 @@
     pick = (row_id == lax.rem(l * vecs + col_id // TILE, columns)).astype(F32)
     noise_part = exact_dot(table, pick)
 
-    pass_2x[0].wait_recv()
-    pass_5 = pass_on(row(1, 3), "A1", up)
-    pass_3x[0].wait_recv()
-    pass_6 = pass_on(row(1, 1), "B1", down)
-    pass_2[0].wait_recv()
-    pass_7a = pass_on(row(0, 2), "A2", across)
-    pass_3[0].wait_recv()
-    pass_7b = pass_on(row(0, 2), "B2", across)
+    pass_2x.wait_recv()
+    pass_5 = pass_on(row(1, 3), "A", up)
+    pass_3x.wait_recv()
+    pass_6 = pass_on(row(1, 1), "B", down)
 
     for s in range(2):
         for d in range(1 - s, 8):
@@ -201,7 +242,7 @@
     def operator_of(shard):
         lanes = slice(shard * nrow, (shard + 1) * nrow)
 
-        @pl.loop(0, whole)
+        @pl.loop(0, whole, unroll=whole)
         def _(block):
             rows = pl.ds(pl.multiple_of(block * TILE, TILE), TILE)
             both = jnp.concatenate(
@@ -219,37 +260,37 @@
             oper[shard, :, rows, :] = result.reshape(walkers, left, nrow).astype(BF16)
 
     loads[3].wait()
-    done = 0
-    for i, copy in enumerate(fac_copies):
+    for copy in fac_copies:
         copy.wait_recv()
-        while done < 8 and (done + 1) * nrow <= FAC_CUTS[i + 1]:
-            operator_of(done)
-            done += 1
-
-    def apply(shard, first):
+    for shard in range(8):
+        operator_of(shard)
+
+    def apply(shards, first):
         for w in range(walkers):
-            product = jnp.dot(
-                oper[shard, w, 0:nrow, :],
-                buf[shard, :, w * nocc : (w + 1) * nocc],
-                preferred_element_type=F32,
-            )
-            out[w] = product if first else out[w] + product
-
-    apply(r, True)
-    for copy in (up_b, down_a, *pass_2[1:], *pass_3[1:], pass_4m, pass_4p, *pass_2x[1:], *pass_3x[1:]):
+            lanes = slice(w * nocc, (w + 1) * nocc)
+            total = None if first else out[w]
+            for shard in shards:
+                product = jnp.dot(oper[shard, w], buf[shard, :, lanes], preferred_element_type=F32)
+                total = product if total is None else total + product
+            out[w] = total
+
+    for copy in (up_b, down_a, pass_4m, pass_4p):
         copy.wait_recv()
-
-    @pl.loop(1, 7)
-    def _(step):
-        over = step // 4
-        along = lax.rem(step, 4) + step // 6
-        apply(row(over, along), False)
-
-    for copy in (pass_5, pass_6, pass_7a, pass_7b):
+    apply((r, row(0, 1), row(0, 3), row(1, 0)), True)
+    for copy in (pass_2, pass_3):
         copy.wait_recv()
-    apply(row(1, 2), False)
+    apply((row(0, 2), row(1, 1), row(1, 3)), False)
+    for copy in (pass_5, pass_6):
+        copy.wait_recv()
+    apply((row(1, 2),), False)
     for copy in sends:
         copy.wait_send()
+    for copy in fac_copies:
+        copy.wait_send()
+
+    @pl.when(is_relay)
+    def _():
+        relayed(1).wait_send()
 
 
 def body(start_pos, field_noise, green_half, orbitals, rotated, factors):
@@ -273,16 +314,18 @@
             pltpu.VMEM((vecs, nocc, width), BF16),
             pltpu.VMEM((vecs, nrow, norb), BF16),
             pltpu.VMEM((vecs, nrow, norb), BF16),
+            pltpu.VMEM((vecs // PARTS, nrow, norb), BF16),
             pltpu.VMEM((8, walkers, nrow, nrow), BF16),
             pltpu.VMEM((walkers * TILE, 2 * vecs * TILE), BF16),
             pltpu.VMEM((walkers * left, 2 * vecs * left), BF16),
             pltpu.VMEM((2, walkers, LANE), F32),
             pltpu.VMEM((2, 8, walkers, LANE), F32),
             dma((4,)),
-            dma((24,)),
-            dma((24,)),
-            dma((4,)),
-            dma((4,)),
+            dma((14,)),
+            dma((14,)),
+            dma((PARTS,)),
+            dma((PARTS,)),
+            dma((2,)),
             dma((2,)),
             dma((2, 8)),
             dma((2, 8)),

time: 162 us -> 116 us (0.72)
  the two profiles are of different devices: /device:TPU:230 before, /device:TPU:225 now
where the time goes in v2:
time: 116 us; the launch traced here: 115 us
  Pallas kernels  112 us (97%)
  local copies, waits for them, and re-layouts  3.89 us (3%)
    pallas_call x1, Pallas kernels, body(): pl.pallas_call(functools.partial(kernel, peers), out_shape=jax.ShapeDtype...  112 us
    unnamed x1, local copies, waits for them, and re-layouts  3.89 us

profile of v2, /device:TPU:225, one launch (start us, length us, event | category | flops | bytes accessed | tf_op | source)
XLA Modules:
  0.0 115.5 jit_solution(13930898375641215933)
XLA Ops:
  0.0 111.6 %shard_map.64 = f32[16,200,200]{2,1,0:T(8,128)} custom-call(s32[32]{0:T(128)} %start_pos.1, f32[32,16,256]{2,1,0:T(8,128)} %noise.1, bf16[16,200,200]{2,1,0:T(8,128)(2,1)} %green.1, bf16[16,200,200]{2,1,0:T(8,128)(2,1)} %orb.1, bf16[8,200,200]{2,1,0:T(8,128)(2,1)} %rot.1, bf16[8,200,1600]{2,1,0:T(8,128)(2,1)} %fac.1), custom_call_target="tpu_custom_call" | custom-call | flops 8192000000 | bytes 20000000 | tf_op jit(solution)/shard_map/pallas_call | solution.py:304
  111.6 3.9 %copy.8 = f32[16,200,200]{2,1,0:T(8,128)} copy(f32[16,200,200]{2,1,0:T(8,128)} %shard_map.64) | data formatting | bytes 5120000

commit v3 on v2

--- a/solution.py
+++ b/solution.py
@@ -11,8 +11,10 @@
 F32, BF16 = jnp.float32, jnp.bfloat16
 EXACT = lax.Precision.HIGHEST
 LANE, TILE = 128, 16
-PARTS = 4
-RELAY_Z = (0, 3, 4)
+CUTS = (0, 384, 1024, 1600)
+ORDER = (0, 1, 2)
+ROUND, HERE, MID = 0, 1, 2
+LEGS = 4
 
 
 def same_slot(rows, cols, width):
@@ -29,6 +31,21 @@
 
 def exact_dot(a, b):
     return lax.dot_general(a, b, (((1,), (0,)), ((), ())), precision=EXACT, preferred_element_type=F32)
+
+
+class Several:
+    def __init__(self, whole, parts):
+        self.whole, self.parts = whole, parts
+
+    def start(self):
+        for part in self.parts:
+            part.start()
+
+    def wait_recv(self):
+        self.whole().wait_recv()
+
+    def wait_send(self):
+        self.whole().wait_send()
 
 
 def partial_bias(green, rot):
@@ -43,7 +60,7 @@
         b = rot[:, rows, :].reshape(vecs * TILE, width)
         return total + lax.dot_general(a, b, (((1,), (1,)), ((), ())), preferred_element_type=F32)
 
-    total = lax.fori_loop(0, whole, step, jnp.zeros((walkers * TILE, vecs * TILE), F32))
+    total = lax.fori_loop(0, whole, step, jnp.zeros((walkers * TILE, vecs * TILE), F32), unroll=True)
     total = jnp.where(same_slot(walkers * TILE, vecs * TILE, TILE), total, 0.0)
     bias = exact_dot(total.reshape(walkers, TILE, vecs * TILE).sum(1), group_sum(vecs * TILE, TILE))
     if left:
@@ -57,8 +74,8 @@
 
 def kernel(
     peers, start_pos, noise, green, orb, rot, fac, out,
-    buf, orb_own, green_own, green_in, rot_own, fac_own, fac_in, fac_relay, oper, mix, mix_left, part, bias,
-    own_sem, ag_send, ag_recv, fac_send, fac_recv, relay_sem, green_sem, bias_send, bias_recv,
+    buf, orb_own, green_own, rot_own, rot_in, fac_own, fac_in, relay, oper, mix, mix_left, part, bias,
+    own_sem, ag_send, ag_recv, fac_send, fac_recv, relay_send, relay_recv, rot_sem, bias_send, bias_recv,
 ):
     walkers, nrow, nocc = orb_own.shape
     vecs = rot_own.shape[0]
@@ -74,8 +91,8 @@
     turn = peers // 2
     near, far = (l // turn) * turn, lax.rem((l // turn) * turn + turn, peers)
     place = lax.rem(l, turn)
-    is_source, is_last = place == 0, place == turn - 1
-    is_relay = functools.reduce(jnp.logical_or, [place == 2 * z for z in RELAY_Z])
+    mid, last = turn // 2, turn - 2
+    is_source, is_mid, is_round, is_last = [place == at for at in (0, mid, last, turn - 1)]
 
     loads = [
         pltpu.make_async_copy(src, dst, own_sem.at[i])
@@ -89,23 +106,29 @@
     barrier = pltpu.get_barrier_semaphore()
     for d in range(1, 8):
         pl.semaphore_signal(barrier, inc=1, device_id=(l, lax.rem(r + d, 8)), device_id_type=MESH)
-    for d in range(8):
-        pl.semaphore_signal(barrier, inc=1, device_id=(after, lax.rem(r + d, 8)), device_id_type=MESH)
-    pl.semaphore_signal(barrier, inc=1, device_id=(before, r), device_id_type=MESH)
-
-    @pl.when(is_relay)
-    def _():
-        pl.semaphore_signal(barrier, inc=1, device_id=(far, r), device_id_type=MESH)
+    pl.semaphore_signal(barrier, inc=1, device_id=(after, r), device_id_type=MESH)
+
+    def greet(position):
+        pl.semaphore_signal(barrier, inc=1, device_id=(position, r), device_id_type=MESH)
+
+    @pl.when(is_source | is_mid)
+    def _():
+        greet(far)
+
+    @pl.when(is_round)
+    def _():
+        greet(near)
 
     @pl.when(is_last)
     def _():
-        for z in RELAY_Z:
-            pl.semaphore_signal(barrier, inc=1, device_id=(near + 2 * z, r), device_id_type=MESH)
+        greet(near)
+        greet(near + mid)
+        greet(far + last)
 
     loads[0].wait()
     for w in range(walkers):
         buf[r, :, w * nocc : (w + 1) * nocc] = orb_own[w]
-    targets = 16 + jnp.where(is_relay, 1, 0) + jnp.where(is_source, len(RELAY_Z), 0)
+    targets = 8 + jnp.where(is_source, 4, 0) + jnp.where(is_mid | is_round, 1, 0)
     pl.semaphore_wait(barrier, targets)
 
     sends = []
@@ -120,7 +143,8 @@
         return copy
 
     tiles = walkers * nocc // LANE
-    pieces = {"A": (0, (tiles + 1) // 2), "B": ((tiles + 1) // 2, tiles // 2)}
+    top = (tiles + 1) // 2
+    pieces = {"A": (0, top), "B": (top, tiles - top)}
     used = [0]
 
     def pass_on(origin, piece, target):
@@ -130,35 +154,60 @@
         ref = buf.at[origin, :, pl.ds(first * LANE, count * LANE)]
         return send(ref, ref, ag_send.at[i], ag_recv.at[i], target)
 
+    def cut(i):
+        return pl.ds(CUTS[i], CUTS[i + 1] - CUTS[i])
+
+    def fac_copy(i, src, dst, send_sem, recv_sem, target):
+        return pltpu.make_async_remote_copy(
+            src_ref=src, dst_ref=dst, send_sem=send_sem, recv_sem=recv_sem,
+            device_id=(target, r), device_id_type=MESH,
+        )
+
+    def vectors(first, count, i, ref):
+        return ref.at[pl.ds(first, count), :, cut(i)]
+
+    def several(i, src, dst, send_sem, recv_sems, target):
+        def some(first, count, recv_sem):
+            return fac_copy(
+                i, vectors(first, count, i, src), vectors(first, count, i, dst), send_sem, recv_sem, target
+            )
+
+        step = vecs // len(recv_sems)
+        whole = functools.partial(some, 0, vecs, recv_sems[0])
+        return Several(whole, [some(k * step, step, sem) for k, sem in enumerate(recv_sems)])
+
+    def direct(i):
+        return several(i, fac, fac_in, fac_send.at[i], [fac_recv.at[i]], before)
+
+    def first_leg(i, target):
+        return several(i, fac, relay, fac_send.at[i], [relay_recv.at[k] for k in range(LEGS)], target)
+
+    def last_leg(i, target):
+        return several(i, relay, fac_in, relay_send.at[0], [fac_recv.at[i]] * LEGS, target)
+
+    def hand_over(first, last):
+        for here, there in zip(first.parts, last.parts):
+            here.wait_recv()
+            there.start()
+
+    fac_copies = [direct(i) for i in range(len(CUTS) - 1)]
+    to_here, from_here = first_leg(HERE, far), last_leg(HERE, near + turn - 1)
+    to_round, from_round = first_leg(ROUND, near + last), last_leg(ROUND, far + turn - 1)
+    to_mid, from_mid = first_leg(MID, far + mid), last_leg(MID, near + turn - 1)
+
+    rot_copy = send(rot, rot_in, rot_sem.at[0], rot_sem.at[1], (before, r))
+    across_a, across_b = pass_on(r, "A", across), pass_on(r, "B", across)
     up_a, down_b = pass_on(r, "A", up), pass_on(r, "B", down)
-    across_a, across_b = pass_on(r, "A", across), pass_on(r, "B", across)
     up_b, down_a = pass_on(r, "B", up), pass_on(r, "A", down)
-    green_copy = send(green, green_in, green_sem.at[0], green_sem.at[1], (after, r))
-
-    share = vecs // PARTS
-
-    def fac_copy(i, dst, recv_sem, target):
-        return pltpu.make_async_remote_copy(
-            src_ref=fac.at[pl.ds(i * share, share)], dst_ref=dst, send_sem=fac_send.at[i], recv_sem=recv_sem,
-            device_id=target, device_id_type=MESH,
-        )
-
-    def landing(i):
-        return fac_in.at[pl.ds(i * share, share)]
-
-    fac_copies = [fac_copy(i, landing(i), fac_recv.at[i], (before, r)) for i in range(PARTS)]
-
     @pl.when(is_source)
     def _():
-        for i, z in enumerate(RELAY_Z, 1):
-            fac_copy(i, fac_relay, relay_sem.at[0], (far + 2 * z, r)).start()
-
-    fac_copies[0].start()
+        to_round.start()
+        to_mid.start()
 
     @pl.when(jnp.logical_not(is_source))
     def _():
-        for copy in fac_copies[1:]:
-            copy.start()
+        for i in ORDER:
+            fac_copies[i].start()
 
     loads[1].wait()
     loads[2].wait()
@@ -167,35 +216,39 @@
     for d in range(1, 8):
         send(part.at[0], bias.at[0, r], bias_send.at[0, d], bias_recv.at[0, r], (l, lax.rem(r + d, 8)))
 
+    rot_copy.wait_recv()
+    part[1] = partial_bias(green_own, rot_in)
+    bias[1, r] = part[1]
+    for d in range(1, 8):
+        send(part.at[1], bias.at[1, r], bias_send.at[1, d], bias_recv.at[1, r], (l, lax.rem(r + d, 8)))
+    out[...] = jnp.zeros_like(out)
+
     up_a.wait_recv()
-    pass_2, pass_2x = pass_on(row(0, 3), "A", up), pass_on(row(0, 3), "A", across)
+    pass_2 = pass_on(row(0, 3), "A", up)
     down_b.wait_recv()
-    pass_3, pass_3x = pass_on(row(0, 1), "B", down), pass_on(row(0, 1), "B", across)
+    pass_3 = pass_on(row(0, 1), "B", down)
+    @pl.when(is_source)
+    def _():
+        to_here.start()
+
+    @pl.when(is_round)
+    def _():
+        hand_over(to_round, from_round)
+
+    across_b.wait_recv()
+    pass_4p = pass_on(row(1, 0), "B", up)
     across_a.wait_recv()
     pass_4m = pass_on(row(1, 0), "A", down)
-    across_b.wait_recv()
-    pass_4p = pass_on(row(1, 0), "B", up)
-
-    def relayed(i):
-        return pltpu.make_async_remote_copy(
-            src_ref=fac_relay, dst_ref=landing(i), send_sem=relay_sem.at[1], recv_sem=fac_recv.at[i],
-            device_id=(near + turn - 1, r), device_id_type=MESH,
-        )
-
-    @pl.when(is_relay)
-    def _():
-        fac_copy(1, fac_relay, relay_sem.at[0], across).wait_recv()
-
-    for i, z in enumerate(RELAY_Z, 1):
-
-        @pl.when(place == 2 * z)
-        def _():
-            relayed(i).start()
-
-    green_copy.wait_recv()
-    part[1] = partial_bias(green_in, rot_own)
-    for d in range(8):
-        send(part.at[1], bias.at[1, r], bias_send.at[1, d], bias_recv.at[1, r], (before, lax.rem(r + d, 8)))
+
+    pass_2x, pass_3x = pass_on(row(0, 3), "A", across), pass_on(row(0, 1), "B", across)
+
+    @pl.when(is_source)
+    def _():
+        hand_over(to_here, from_here)
+
+    @pl.when(is_mid)
+    def _():
+        hand_over(to_mid, from_mid)
 
     block = jnp.int32(0)
     for k in range(peers):
@@ -207,13 +260,12 @@
     pick = (row_id == lax.rem(l * vecs + col_id // TILE, columns)).astype(F32)
     noise_part = exact_dot(table, pick)
 
-    pass_2x.wait_recv()
-    pass_5 = pass_on(row(1, 3), "A", up)
-    pass_3x.wait_recv()
-    pass_6 = pass_on(row(1, 1), "B", down)
-
+    pass_4p.wait_recv()
+    pass_5 = pass_on(row(1, 3), "B", up)
+    pass_4m.wait_recv()
+    pass_6 = pass_on(row(1, 1), "A", down)
     for s in range(2):
-        for d in range(1 - s, 8):
+        for d in range(1, 8):
             j = lax.rem(r + d, 8)
             pltpu.make_async_remote_copy(
                 src_ref=part.at[s], dst_ref=bias.at[s, j], send_sem=bias_send.at[s, d],
@@ -259,38 +311,61 @@
             result = jnp.dot(mix_left[...], both, preferred_element_type=F32)
             oper[shard, :, rows, :] = result.reshape(walkers, left, nrow).astype(BF16)
 
-    loads[3].wait()
-    for copy in fac_copies:
-        copy.wait_recv()
-    for shard in range(8):
-        operator_of(shard)
-
-    def apply(shards, first):
+    def apply(shards):
         for w in range(walkers):
             lanes = slice(w * nocc, (w + 1) * nocc)
-            total = None if first else out[w]
+            total = out[w]
             for shard in shards:
-                product = jnp.dot(oper[shard, w], buf[shard, :, lanes], preferred_element_type=F32)
-                total = product if total is None else total + product
+                total += jnp.dot(oper[shard, w], buf[shard, :, lanes], preferred_element_type=F32)
             out[w] = total
 
-    for copy in (up_b, down_a, pass_4m, pass_4p):
+    for copy in (up_b, down_a):
         copy.wait_recv()
-    apply((r, row(0, 1), row(0, 3), row(1, 0)), True)
-    for copy in (pass_2, pass_3):
+    loads[3].wait()
+    seen = [False] * len(ORDER)
+    done = set()
+    for i in ORDER:
+        fac_copies[i].wait_recv()
+        seen[i] = True
+        ready = []
+        for shard in range(8):
+            parts = [k for k in range(len(ORDER)) if CUTS[k] < (shard + 1) * nrow and CUTS[k + 1] > shard * nrow]
+            if shard not in done and all(seen[k] for k in parts):
+                ready.append(shard)
+                operator_of(shard)
+        done.update(ready)
+
+        @pl.loop(ready[0], ready[-1] + 1)
+        def _(shard):
+            along = lax.rem(shard % 4 - y + 4, 4)
+            early = jnp.where(shard // 4 == half, along != 2, along == 0)
+
+            @pl.when(early)
+            def _():
+                apply((shard,))
+
+    for copy in (pass_2x, pass_3x, pass_2, pass_3):
         copy.wait_recv()
-    apply((row(0, 2), row(1, 1), row(1, 3)), False)
+    apply((row(0, 2), row(1, 1), row(1, 3)))
     for copy in (pass_5, pass_6):
         copy.wait_recv()
-    apply((row(1, 2),), False)
+    apply((row(1, 2),))
     for copy in sends:
         copy.wait_send()
     for copy in fac_copies:
         copy.wait_send()
 
-    @pl.when(is_relay)
-    def _():
-        relayed(1).wait_send()
+    @pl.when(is_source)
+    def _():
+        from_here.wait_send()
+
+    @pl.when(is_round)
+    def _():
+        from_round.wait_send()
+
+    @pl.when(is_mid)
+    def _():
+        from_mid.wait_send()
 
 
 def body(start_pos, field_noise, green_half, orbitals, rotated, factors):
@@ -310,11 +385,11 @@
             pltpu.VMEM((8, nrow, walkers * nocc), BF16),
             pltpu.VMEM((walkers, nrow, nocc), BF16),
             pltpu.VMEM((walkers, nocc, width), BF16),
-            pltpu.VMEM((walkers, nocc, width), BF16),
+            pltpu.VMEM((vecs, nocc, width), BF16),
             pltpu.VMEM((vecs, nocc, width), BF16),
             pltpu.VMEM((vecs, nrow, norb), BF16),
             pltpu.VMEM((vecs, nrow, norb), BF16),
-            pltpu.VMEM((vecs // PARTS, nrow, norb), BF16),
+            pltpu.VMEM((vecs, nrow, norb), BF16),
             pltpu.VMEM((8, walkers, nrow, nrow), BF16),
             pltpu.VMEM((walkers * TILE, 2 * vecs * TILE), BF16),
             pltpu.VMEM((walkers * left, 2 * vecs * left), BF16),
@@ -323,9 +398,10 @@
             dma((4,)),
             dma((14,)),
             dma((14,)),
-            dma((PARTS,)),
-            dma((PARTS,)),
-            dma((2,)),
+            dma((len(ORDER),)),
+            dma((len(ORDER),)),
+            dma((1,)),
+            dma((LEGS,)),
             dma((2,)),
             dma((2, 8)),
             dma((2, 8)),

time: 116 us -> 96.8 us (0.83)
  the two profiles are of different devices: /device:TPU:225 before, /device:TPU:230 now
where the time goes in v3:
time: 96.8 us; the launch traced here: 95.2 us
  Pallas kernels  91.3 us (94%)
  local copies, waits for them, and re-layouts  3.89 us (4%)
    pallas_call x1, Pallas kernels, body(): pl.pallas_call(functools.partial(kernel, peers), out_shape=jax.ShapeDtype...  91.3 us
    unnamed x1, local copies, waits for them, and re-layouts  3.89 us

profile of v3, /device:TPU:230, one launch (start us, length us, event | category | flops | bytes accessed | tf_op | source)
XLA Modules:
  0.0 95.2 jit_solution(15787357513291227591)
XLA Ops:
  0.0 91.3 %shard_map.64 = f32[16,200,200]{2,1,0:T(8,128)} custom-call(s32[32]{0:T(128)} %start_pos.1, f32[32,16,256]{2,1,0:T(8,128)} %noise.1, bf16[16,200,200]{2,1,0:T(8,128)(2,1)} %green.1, bf16[16,200,200]{2,1,0:T(8,128)(2,1)} %orb.1, bf16[8,200,200]{2,1,0:T(8,128)(2,1)} %rot.1, bf16[8,200,1600]{2,1,0:T(8,128)(2,1)} %fac.1), custom_call_target="tpu_custom_call" | custom-call | flops 8192000000 | bytes 20000000 | tf_op jit(solution)/shard_map/pallas_call | solution.py:379
  91.3 3.9 %copy.8 = f32[16,200,200]{2,1,0:T(8,128)} copy(f32[16,200,200]{2,1,0:T(8,128)} %shard_map.64) | data formatting | bytes 5120000

commit v4 on v3

--- a/solution.py
+++ b/solution.py
@@ -11,9 +11,9 @@
 F32, BF16 = jnp.float32, jnp.bfloat16
 EXACT = lax.Precision.HIGHEST
 LANE, TILE = 128, 16
-CUTS = (0, 384, 1024, 1600)
-ORDER = (0, 1, 2)
-ROUND, HERE, MID = 0, 1, 2
+CUTS = (0, 256, 640, 1152, 1600)
+ORDER = (0, 2, 3, 1)
+ROUND, LATE, HERE, MID = 0, 1, 2, 3
 LEGS = 4
 
 
@@ -91,8 +91,10 @@
     turn = peers // 2
     near, far = (l // turn) * turn, lax.rem((l // turn) * turn + turn, peers)
     place = lax.rem(l, turn)
-    mid, last = turn // 2, turn - 2
-    is_source, is_mid, is_round, is_last = [place == at for at in (0, mid, last, turn - 1)]
+    hop, mid, late, last = turn // 4, turn // 2, turn - 4, turn - 2
+    is_source, is_hop, is_mid, is_late, is_round, is_last = [
+        place == at for at in (0, hop, mid, late, last, turn - 1)
+    ]
 
     loads = [
         pltpu.make_async_copy(src, dst, own_sem.at[i])
@@ -115,20 +117,25 @@
     def _():
         greet(far)
 
-    @pl.when(is_round)
+    @pl.when(is_round | is_hop)
     def _():
         greet(near)
+
+    @pl.when(is_late)
+    def _():
+        greet(far + hop)
 
     @pl.when(is_last)
     def _():
         greet(near)
         greet(near + mid)
+        greet(near + late)
         greet(far + last)
 
     loads[0].wait()
     for w in range(walkers):
         buf[r, :, w * nocc : (w + 1) * nocc] = orb_own[w]
-    targets = 8 + jnp.where(is_source, 4, 0) + jnp.where(is_mid | is_round, 1, 0)
+    targets = 8 + jnp.where(is_source, 5, 0) + jnp.where(is_hop | is_mid | is_late | is_round, 1, 0)
     pl.semaphore_wait(barrier, targets)
 
     sends = []
@@ -144,7 +151,11 @@
 
     tiles = walkers * nocc // LANE
     top = (tiles + 1) // 2
-    pieces = {"A": (0, top), "B": (top, tiles - top)}
+    mid_a, mid_b = (top + 1) // 2, (top + tiles) // 2
+    pieces = {
+        "A": (0, top), "A1": (0, mid_a), "A2": (mid_a, top - mid_a),
+        "B": (top, tiles - top), "B1": (top, mid_b - top), "B2": (mid_b, tiles - mid_b),
+    }
     used = [0]
 
     def pass_on(origin, piece, target):
@@ -185,6 +196,9 @@
     def last_leg(i, target):
         return several(i, relay, fac_in, relay_send.at[0], [fac_recv.at[i]] * LEGS, target)
 
+    def next_leg(i, target):
+        return several(i, relay, relay, relay_send.at[0], [relay_recv.at[k] for k in range(LEGS)], target)
+
     def hand_over(first, last):
         for here, there in zip(first.parts, last.parts):
             here.wait_recv()
@@ -193,6 +207,7 @@
     fac_copies = [direct(i) for i in range(len(CUTS) - 1)]
     to_here, from_here = first_leg(HERE, far), last_leg(HERE, near + turn - 1)
     to_round, from_round = first_leg(ROUND, near + last), last_leg(ROUND, far + turn - 1)
+    to_hop, to_late, from_late = first_leg(LATE, near + hop), next_leg(LATE, far + late), last_leg(LATE, near + turn - 1)
     to_mid, from_mid = first_leg(MID, far + mid), last_leg(MID, near + turn - 1)
 
     rot_copy = send(rot, rot_in, rot_sem.at[0], rot_sem.at[1], (before, r))
@@ -202,12 +217,16 @@
     @pl.when(is_source)
     def _():
         to_round.start()
+        to_hop.start()
         to_mid.start()
 
-    @pl.when(jnp.logical_not(is_source))
-    def _():
-        for i in ORDER:
-            fac_copies[i].start()
+    def send_parts(*parts):
+        @pl.when(jnp.logical_not(is_source))
+        def _():
+            for i in parts:
+                fac_copies[i].start()
+
+    send_parts(*ORDER[:2])
 
     loads[1].wait()
     loads[2].wait()
@@ -227,6 +246,7 @@
     pass_2 = pass_on(row(0, 3), "A", up)
     down_b.wait_recv()
     pass_3 = pass_on(row(0, 1), "B", down)
+    send_parts(ORDER[2])
     @pl.when(is_source)
     def _():
         to_here.start()
@@ -235,11 +255,16 @@
     def _():
         hand_over(to_round, from_round)
 
+    @pl.when(is_hop)
+    def _():
+        hand_over(to_hop, to_late)
+
     across_b.wait_recv()
-    pass_4p = pass_on(row(1, 0), "B", up)
+    pass_4p = pass_on(row(1, 0), "B1", up), pass_on(row(1, 0), "B2", up)
     across_a.wait_recv()
-    pass_4m = pass_on(row(1, 0), "A", down)
-
+    pass_4m = pass_on(row(1, 0), "A1", down), pass_on(row(1, 0), "A2", down)
+
+    send_parts(ORDER[3])
     pass_2x, pass_3x = pass_on(row(0, 3), "A", across), pass_on(row(0, 1), "B", across)
 
     @pl.when(is_source)
@@ -249,6 +274,10 @@
     @pl.when(is_mid)
     def _():
         hand_over(to_mid, from_mid)
+
+    @pl.when(is_late)
+    def _():
+        hand_over(to_late, from_late)
 
     block = jnp.int32(0)
     for k in range(peers):
@@ -260,10 +289,13 @@
     pick = (row_id == lax.rem(l * vecs + col_id // TILE, columns)).astype(F32)
     noise_part = exact_dot(table, pick)
 
-    pass_4p.wait_recv()
-    pass_5 = pass_on(row(1, 3), "B", up)
-    pass_4m.wait_recv()
-    pass_6 = pass_on(row(1, 1), "A", down)
+    final = []
+    for i in range(2):
+        pass_4p[i].wait_recv()
+        final.append(pass_on(row(1, 3), ("B1", "B2")[i], up))
+        pass_4m[i].wait_recv()
+        final.append(pass_on(row(1, 1), ("A1", "A2")[i], down))
+
     for s in range(2):
         for d in range(1, 8):
             j = lax.rem(r + d, 8)
@@ -347,7 +379,7 @@
     for copy in (pass_2x, pass_3x, pass_2, pass_3):
         copy.wait_recv()
     apply((row(0, 2), row(1, 1), row(1, 3)))
-    for copy in (pass_5, pass_6):
+    for copy in final:
         copy.wait_recv()
     apply((row(1, 2),))
     for copy in sends:
@@ -362,6 +394,14 @@
     @pl.when(is_round)
     def _():
         from_round.wait_send()
+
+    @pl.when(is_hop)
+    def _():
+        to_late.wait_send()
+
+    @pl.when(is_late)
+    def _():
+        from_late.wait_send()
 
     @pl.when(is_mid)
     def _():
@@ -396,8 +436,8 @@
             pltpu.VMEM((2, walkers, LANE), F32),
             pltpu.VMEM((2, 8, walkers, LANE), F32),
             dma((4,)),
-            dma((14,)),
-            dma((14,)),
+            dma((18,)),
+            dma((18,)),
             dma((len(ORDER),)),
             dma((len(ORDER),)),
             dma((1,)),

time: 96.8 us -> 92.6 us (0.957)
  Pallas kernels: 91.3 us -> 87.1 us
    pallas_call x1, Pallas kernels: 91.3 us -> 87.1 us  [body(): pl.pallas_call(functools.partial(kernel, peers), out_shape=jax.ShapeDtype...]
where the time goes in v4:
time: 92.6 us; the launch traced here: 90.9 us
  Pallas kernels  87.1 us (94%)
  local copies, waits for them, and re-layouts  3.89 us (4%)
    pallas_call x1, Pallas kernels, body(): pl.pallas_call(functools.partial(kernel, peers), out_shape=jax.ShapeDtype...  87.1 us
    unnamed x1, local copies, waits for them, and re-layouts  3.89 us

profile of v4, /device:TPU:230, one launch (start us, length us, event | category | flops | bytes accessed | tf_op | source)
XLA Modules:
  0.0 90.9 jit_solution(9366192918134635920)
XLA Ops:
  0.0 87.1 %shard_map.64 = f32[16,200,200]{2,1,0:T(8,128)} custom-call(s32[32]{0:T(128)} %start_pos.1, f32[32,16,256]{2,1,0:T(8,128)} %noise.1, bf16[16,200,200]{2,1,0:T(8,128)(2,1)} %green.1, bf16[16,200,200]{2,1,0:T(8,128)(2,1)} %orb.1, bf16[8,200,200]{2,1,0:T(8,128)(2,1)} %rot.1, bf16[8,200,1600]{2,1,0:T(8,128)(2,1)} %fac.1), custom_call_target="tpu_custom_call" | custom-call | flops 8192000000 | bytes 20000000 | tf_op jit(solution)/shard_map/pallas_call | solution.py:419
  87.1 3.9 %copy.8 = f32[16,200,200]{2,1,0:T(8,128)} copy(f32[16,200,200]{2,1,0:T(8,128)} %shard_map.64) | data formatting | bytes 5120000

commit v5 on v4

--- a/solution.py
+++ b/solution.py
@@ -288,13 +288,6 @@
     col_id = lax.broadcasted_iota(jnp.int32, (columns, 2 * vecs * TILE), 1)
     pick = (row_id == lax.rem(l * vecs + col_id // TILE, columns)).astype(F32)
     noise_part = exact_dot(table, pick)
-
-    final = []
-    for i in range(2):
-        pass_4p[i].wait_recv()
-        final.append(pass_on(row(1, 3), ("B1", "B2")[i], up))
-        pass_4m[i].wait_recv()
-        final.append(pass_on(row(1, 1), ("A1", "A2")[i], down))
 
     for s in range(2):
         for d in range(1, 8):
@@ -351,12 +344,19 @@
                 total += jnp.dot(oper[shard, w], buf[shard, :, lanes], preferred_element_type=F32)
             out[w] = total
 
-    for copy in (up_b, down_a):
+    for copy in (up_b, down_a, pass_2, pass_3):
         copy.wait_recv()
     loads[3].wait()
     seen = [False] * len(ORDER)
     done = set()
     for i in ORDER:
+        if i == ORDER[2]:
+            final = []
+            for n in range(2):
+                pass_4p[n].wait_recv()
+                final.append(pass_on(row(1, 3), ("B1", "B2")[n], up))
+                pass_4m[n].wait_recv()
+                final.append(pass_on(row(1, 1), ("A1", "A2")[n], down))
         fac_copies[i].wait_recv()
         seen[i] = True
         ready = []
@@ -370,15 +370,15 @@
         @pl.loop(ready[0], ready[-1] + 1)
         def _(shard):
             along = lax.rem(shard % 4 - y + 4, 4)
-            early = jnp.where(shard // 4 == half, along != 2, along == 0)
+            early = (shard // 4 == half) | (along == 0)
 
             @pl.when(early)
             def _():
                 apply((shard,))
 
-    for copy in (pass_2x, pass_3x, pass_2, pass_3):
+    for copy in (pass_2x, pass_3x):
         copy.wait_recv()
-    apply((row(0, 2), row(1, 1), row(1, 3)))
+    apply((row(1, 1), row(1, 3)))
     for copy in final:
         copy.wait_recv()
     apply((row(1, 2),))

time: 92.6 us -> 92.1 us (level)
  no operation moved by 1% of the time
where the time goes in v5:
time: 92.1 us; the launch traced here: 90.3 us
  Pallas kernels  86.4 us (94%)
  local copies, waits for them, and re-layouts  3.89 us (4%)
    pallas_call x1, Pallas kernels, body(): pl.pallas_call(functools.partial(kernel, peers), out_shape=jax.ShapeDtype...  86.4 us
    unnamed x1, local copies, waits for them, and re-layouts  3.89 us

profile of v5, /device:TPU:230, one launch (start us, length us, event | category | flops | bytes accessed | tf_op | source)
XLA Modules:
  0.0 90.3 jit_solution(10848809176922948689)
XLA Ops:
  0.0 86.4 %shard_map.64 = f32[16,200,200]{2,1,0:T(8,128)} custom-call(s32[32]{0:T(128)} %start_pos.1, f32[32,16,256]{2,1,0:T(8,128)} %noise.1, bf16[16,200,200]{2,1,0:T(8,128)(2,1)} %green.1, bf16[16,200,200]{2,1,0:T(8,128)(2,1)} %orb.1, bf16[8,200,200]{2,1,0:T(8,128)(2,1)} %rot.1, bf16[8,200,1600]{2,1,0:T(8,128)(2,1)} %fac.1), custom_call_target="tpu_custom_call" | custom-call | flops 8192000000 | bytes 20000000 | tf_op jit(solution)/shard_map/pallas_call | solution.py:419
  86.5 3.9 %copy.8 = f32[16,200,200]{2,1,0:T(8,128)} copy(f32[16,200,200]{2,1,0:T(8,128)} %shard_map.64) | data formatting | bytes 5120000
